TPU v7x, 32 devices: a whole 2x2x4 slice. The times are simulated.
32 devices in a mesh: row: 4 (over z), col: 4 (over y, x), dp: 2 (over core).
Axes of the slice: x: 2, y: 2, z: 4, core: 2. Of those that a mesh axis runs over, the one named last changes fastest.
Arguments:
- tokens: bfloat16 [128, 8192], P(('col', 'dp'), 'row'), may hold values from -6 to 6
- grad_out: bfloat16 [128, 8192], P(('col', 'dp'), 'row'), may hold values from -1.1953125 to 1.1953125
- gate_weight: bfloat16 [8192, 16384], P('row', 'col'), may hold values from -0.0625 to 0.0625
- up_weight: bfloat16 [8192, 16384], P('row', 'col'), may hold values from -0.0625 to 0.0625
- down_weight: bfloat16 [16384, 8192], P('col', 'row'), may hold values from -0.046875 to 0.046875
Outputs:
- grad_tokens: bfloat16 [128, 8192], P(('col', 'dp'), 'row')
- grad_gate: bfloat16 [8192, 16384], P('row', ('col', 'dp'))
- grad_up: bfloat16 [8192, 16384], P('row', ('col', 'dp'))
- grad_down: bfloat16 [16384, 8192], P(('col', 'dp'), 'row')
All inputs are finite; a program needn't handle non-finite values.
Results may differ from a plain program's by a relative error of at most 0.0049.
Values may be sent and summed in bfloat16 or wider, within the bound.
A program may use at most 128 MiB of HBM per device.

v0:
```python
import jax
import jax.numpy as jnp
from jax import lax
from jax.sharding import PartitionSpec as P


def swiglu_back(gate, up, grad_hidden):
    sig = jax.nn.sigmoid(gate)
    hidden = (gate * sig * up).astype(jnp.bfloat16)
    grad_g = (grad_hidden * up * sig * (1.0 + gate * (1.0 - sig))).astype(jnp.bfloat16)
    grad_u = (grad_hidden * gate * sig).astype(jnp.bfloat16)
    return (hidden, grad_g, grad_u)


def body(tokens, grad_out, gate_weight, up_weight, down_weight):
    contract_last = (((1,), (1,)), ((), ()))
    contract_first = (((0,), (0,)), ((), ()))
    panel_in, panel_grad = (
        lax.all_gather(tokens, "col", axis=0, tiled=True),
        lax.all_gather(grad_out, "col", axis=0, tiled=True),
    )
    gate_part = jnp.dot(panel_in, gate_weight, preferred_element_type=jnp.float32)
    up_part = jnp.dot(panel_in, up_weight, preferred_element_type=jnp.float32)
    hidden_part = lax.dot_general(
        panel_grad, down_weight, contract_last, preferred_element_type=jnp.float32
    )
    gate, up, grad_hidden = lax.psum((gate_part, up_part, hidden_part), "row")
    hidden, grad_g, grad_u = swiglu_back(gate, up, grad_hidden)
    total = lax.dot_general(grad_g, gate_weight, contract_last, preferred_element_type=jnp.float32)
    grad_tokens = lax.psum_scatter(
        total
        + lax.dot_general(grad_u, up_weight, contract_last, preferred_element_type=jnp.float32),
        "col",
        scatter_dimension=0,
        tiled=True,
    ).astype(jnp.bfloat16)
    both_in, both_grad = (
        lax.all_gather(panel_in, "dp", axis=0, tiled=True),
        lax.all_gather(panel_grad, "dp", axis=0, tiled=True),
    )
    both_g, both_u, both_h = (
        lax.all_to_all(grad_g, "dp", split_axis=1, concat_axis=0, tiled=True),
        lax.all_to_all(grad_u, "dp", split_axis=1, concat_axis=0, tiled=True),
        lax.all_to_all(hidden, "dp", split_axis=1, concat_axis=0, tiled=True),
    )
    grad_gate = lax.dot_general(both_in, both_g, contract_first, preferred_element_type=jnp.float32)
    grad_up = lax.dot_general(both_in, both_u, contract_first, preferred_element_type=jnp.float32)
    grad_down = lax.dot_general(
        both_h, both_grad, contract_first, preferred_element_type=jnp.float32
    )
    return (
        grad_tokens,
        grad_gate.astype(jnp.bfloat16),
        grad_up.astype(jnp.bfloat16),
        grad_down.astype(jnp.bfloat16),
    )


def solution(mesh):
    in_specs = (
        P(("col", "dp"), "row"),
        P(("col", "dp"), "row"),
        P("row", "col"),
        P("row", "col"),
        P("col", "row"),
    )
    out_specs = (
        P(("col", "dp"), "row"),
        P("row", ("col", "dp")),
        P("row", ("col", "dp")),
        P(("col", "dp"), "row"),
    )
    return jax.shard_map(body, mesh=mesh, in_specs=in_specs, out_specs=out_specs, check_vma=False)
```

profile of v0, /device:TPU:1, one launch (start us, length us, event | category | flops | bytes accessed | tf_op | source)
XLA Modules:
  0.0 262.9 jit_solution(1236256350307320676)
XLA Ops:
  7.2 0.0 all-reduce.3.cloned.1.call-start
  7.2 0.0 copy-start
  7.2 9.5 %all_gather.13 = bf16[64,2048]{1,0:T(8,128)(2,1)S(1)} all-gather(bf16[16,2048]{1,0:T(8,128)(2,1)} %param.5), channel_id=1, replica_groups=mesh['row'=4,'col'=4,'dp'=2] {'col'}, dimensions={0}, use_global_device_ids=true | all-gather | bytes 327680 | tf_op jit(solution)/shard_map/all_gather | solution.py:19
  16.7 9.8 %fusion.1 = f32[64,4096]{1,0:T(8,128)} fusion(bf16[64,2048]{1,0:T(8,128)(2,1)S(1)} %all_gather.13, bf16[2048,4096]{1,0:T(8,128)(2,1)} %param.8), kind=kOutput, calls=%fused_computation.12 | convolution fusion | flops 1073741824 | bytes 18087936 | tf_op jit(solution)/shard_map/dot_general | solution.py:23
  26.5 0.0 copy-done
  26.5 0.0 copy-start.1
  26.5 4.0 %fusion.2 = f32[64,4096]{1,0:T(8,128)} fusion(bf16[64,2048]{1,0:T(8,128)(2,1)S(1)} %all_gather.13, bf16[2048,4096]{1,0:T(8,128)(2,1)S(1)} %copy-done), kind=kOutput, calls=%fused_computation.13 | convolution fusion | flops 1073741824 | bytes 18087936 | tf_op jit(solution)/shard_map/dot_general | solution.py:22
  30.5 0.0 copy-done.1
  30.5 5.8 %all_gather.12 = bf16[64,2048]{1,0:T(8,128)(2,1)S(1)} all-gather(bf16[16,2048]{1,0:T(8,128)(2,1)S(1)} %copy-done.1), channel_id=1, replica_groups=mesh['row'=4,'col'=4,'dp'=2] {'col'}, dimensions={0}, use_global_device_ids=true | all-gather | bytes 327680 | tf_op jit(solution)/shard_map/all_gather | solution.py:20
  36.3 11.9 %fusion = f32[64,4096]{1,0:T(8,128)} fusion(bf16[64,2048]{1,0:T(8,128)(2,1)S(1)} %all_gather.12, bf16[4096,2048]{1,0:T(8,128)(2,1)} %param.9), kind=kOutput, calls=%fused_computation.11 | convolution fusion | flops 1073741824 | bytes 18087936 | tf_op jit(solution)/shard_map/dot_general | solution.py:24
  48.2 0.0 all-reduce.3.cloned.1.call-update
  48.2 0.0 reduce-scatter.2.cloned.1.call-start
  48.3 6.6 %all_gather.14 = bf16[128,2048]{1,0:T(8,128)(2,1)S(1)} all-gather(bf16[64,2048]{1,0:T(8,128)(2,1)S(1)} %all_gather.13), channel_id=1, replica_groups=mesh['row'=4,'col'=4,'dp'=2] {'dp'}, dimensions={0}, use_global_device_ids=true | all-gather | bytes 786432 | tf_op jit(solution)/shard_map/all_gather | solution.py:38
  54.9 2.3 all_gather.15
  57.2 117.3 %all-reduce.3.cloned.1.call-done = (f32[64,4096]{1,0:T(8,128)}, f32[64,4096]{1,0:T(8,128)}, f32[64,4096]{1,0:T(8,128)}) async-done(((f32[64,4096]{1,0:T(8,128)}, f32[64,4096]{1,0:T(8,128)}, f32[64,4096]{1,0:T(8,128)}), (f32[64,4096]{1,0:T(8,128)}, f32[64,4096]{1,0:T(8,128)}, f32[64,4096]{1,0:T(8,128)})) %all-reduce.3.cloned.1.call-update) | async-done | bytes 3145744 | tf_op jit(solution)/shard_map/psum | solution.py:27
  174.5 2.4 multiply_convert_fusion
  177.0 11.0 %fusion.3 = f32[64,2048]{1,0:T(8,128)S(1)} fusion(bf16[64,4096]{1,0:T(8,128)(2,1)S(1)} %get-tuple-element.16, bf16[2048,4096]{1,0:T(8,128)(2,1)} %param.7), kind=kOutput, calls=%fused_computation.14 | convolution fusion | flops 1073741824 | bytes 17825792 | tf_op jit(solution)/shard_map/dot_general | solution.py:29
  187.9 11.8 %convolution_add_fusion = f32[64,2048]{1,0:T(8,128)} fusion(f32[64,2048]{1,0:T(8,128)S(1)} %fusion.3, bf16[64,4096]{1,0:T(8,128)(2,1)S(1)} %get-tuple-element.17, bf16[2048,4096]{1,0:T(8,128)(2,1)} %param.8), kind=kOutput, calls=%fused_computation.3 | convolution fusion | flops 1073872896 | bytes 18350080 | tf_op jit(solution)/shard_map/dot_general | solution.py:32
  199.7 0.0 reduce-scatter.2.cloned.1.call-update
  199.8 4.5 %all_to_all.57 = bf16[64,2,2048]{2,0,1:T(8,128)(2,1)S(1)} all-to-all(bf16[64,2,2048]{2,0,1:T(8,128)(2,1)S(1)} %bitcast.47), channel_id=1, replica_groups=mesh['row'=4,'col'=4,'dp'=2] {'dp'}, dimensions={1} | all-to-all | bytes 1048576 | tf_op jit(solution)/shard_map/all_to_all | solution.py:42
  204.2 5.8 %convert_bitcast_fusion.1 = bf16[2048,2048]{0,1:T(8,128)(2,1)} fusion(bf16[128,2048]{1,0:T(8,128)(2,1)S(1)} %bitcast.45, bf16[128,2048]{1,0:T(8,128)(2,1)S(1)} %all_gather.14), kind=kOutput, calls=%fused_computation.1 | convolution fusion | flops 1077936128 | bytes 9437184 | tf_op jit(solution)/shard_map/dot_general | solution.py:46
  210.0 12.2 %copy.14 = bf16[2048,2048]{1,0:T(8,128)(2,1)} copy(bf16[2048,2048]{0,1:T(8,128)(2,1)} %convert_bitcast_fusion.1) | data formatting | bytes 16777216
  222.3 4.3 %all_to_all.58 = bf16[64,2,2048]{2,0,1:T(8,128)(2,1)S(1)} all-to-all(bf16[64,2,2048]{2,0,1:T(8,128)(2,1)S(1)} %bitcast.48), channel_id=1, replica_groups=mesh['row'=4,'col'=4,'dp'=2] {'dp'}, dimensions={1} | all-to-all | bytes 1048576 | tf_op jit(solution)/shard_map/all_to_all | solution.py:43
  226.6 5.8 %convert_bitcast_fusion = bf16[2048,2048]{0,1:T(8,128)(2,1)} fusion(bf16[128,2048]{1,0:T(8,128)(2,1)S(1)} %bitcast.43, bf16[128,2048]{1,0:T(8,128)(2,1)S(1)} %all_gather.14), kind=kOutput, calls=%fused_computation | convolution fusion | flops 1077936128 | bytes 9437184 | tf_op jit(solution)/shard_map/dot_general | solution.py:47
  232.4 12.2 %copy.15 = bf16[2048,2048]{1,0:T(8,128)(2,1)} copy(bf16[2048,2048]{0,1:T(8,128)(2,1)} %convert_bitcast_fusion) | data formatting | bytes 16777216
  244.6 4.1 %all_to_all.59 = bf16[64,2,2048]{2,0,1:T(8,128)(2,1)S(1)} all-to-all(bf16[64,2,2048]{2,0,1:T(8,128)(2,1)S(1)} %bitcast.49), channel_id=1, replica_groups=mesh['row'=4,'col'=4,'dp'=2] {'dp'}, dimensions={1} | all-to-all | bytes 1048576 | tf_op jit(solution)/shard_map/all_to_all | solution.py:44
  248.7 5.8 %convolution_convert_fusion = bf16[2048,2048]{1,0:T(8,128)(2,1)} fusion(bf16[128,2048]{1,0:T(8,128)(2,1)S(1)} %bitcast.44, bf16[128,2048]{1,0:T(8,128)(2,1)S(1)} %all_gather.15), kind=kOutput, calls=%fused_computation.2 | convolution fusion | flops 1077936128 | bytes 9437184 | tf_op jit(solution)/shard_map/dot_general | solution.py:48
  254.5 0.0 reduce-scatter.2.cloned.1.call-done
  254.5 1.5 convert_element_type.29
  (3 shorter events, 0.1 us)
Async XLA Ops:
  7.2 167.4 %all-reduce.3.cloned.1.call-start = ((), (), s32[]{:S(2)}) async-start(), calls=%async_computation.5 | async-start | bytes 6291456 | tf_op jit(solution)/shard_map/psum | solution.py:27
  7.2 19.3 %copy-start = (bf16[2048,4096]{1,0:T(8,128)(2,1)S(1)}, bf16[2048,4096]{1,0:T(8,128)(2,1)}, u32[]{:S(2)}) copy-start(bf16[2048,4096]{1,0:T(8,128)(2,1)} %param.7) | copy-start | bytes 50331652
  26.5 4.0 %copy-start.1 = (bf16[16,2048]{1,0:T(8,128)(2,1)S(1)}, bf16[16,2048]{1,0:T(8,128)(2,1)}, u32[]{:S(2)}) copy-start(bf16[16,2048]{1,0:T(8,128)(2,1)} %param.6) | copy-start | bytes 196612
  48.2 206.3 %reduce-scatter.2.cloned.1.call-start = ((), (), s32[]{:S(2)}) async-start(), calls=%async_computation.4 | async-start | bytes 655360 | tf_op jit(solution)/shard_map/reduce_scatter | solution.py:30
Sparse Core Ops, SparseCore 0:
  48.3 126.1 all-reduce.2
  199.8 23.6 reduce-scatter.1
where the time goes:
time: 264 us; the launch traced here: 263 us
  waiting for transfers between devices  117 us (44%)
  matrix products  65.8 us (25%)
  blocking collectives  37 us (14%)
  local copies, waits for them, and re-layouts  24.6 us (9%)
  between operations  14.1 us (5%)
  other arithmetic  3.96 us (2%)
    psum x1, waiting for transfers between devices, body(): gate, up, grad_hidden = lax.psum((gate_part, up_part, hidden_part), 'row')  117 us
    unnamed x6, local copies, waits for them, and re-layouts  24.5 us
    dot_general x1, matrix products, body(): lax.dot_general(panel_grad, down_weight, contract_last, preferred_element...  11.9 us
    dot_general x1, matrix products, body(): lax.dot_general(grad_u, up_weight, contract_last, preferred_element_type=...  11.8 us
    dot_general x1, matrix products, body(): lax.dot_general(grad_g, gate_weight, contract_last, preferred_element_typ...  11 us
    dot_general x1, matrix products, body(): up_part = jnp.dot(panel_in, up_weight, preferred_element_type=jnp.float32)  9.76 us
    all_gather x1, blocking collectives, body(): lax.all_gather(tokens, 'col', axis=0, tiled=True)  9.5 us
    all_gather x1, blocking collectives, body(): lax.all_gather(panel_in, 'dp', axis=0, tiled=True)  6.63 us
  transfers between devices with their start and end apart: 2, of which 1 were waited for; matrix products, arithmetic and copies ran while one was open for 16% of the time, Pallas kernels for 0%

commit v1 on v0

v1 whole, which is shorter than its diff:
```python
import functools

import jax
import jax.numpy as jnp
from jax import lax
from jax.experimental import pallas as pl
from jax.experimental.pallas import tpu as pltpu
from jax.sharding import PartitionSpec as P

MESH = pl.DeviceIdType.MESH
BF16 = jnp.bfloat16
F32 = jnp.float32
NT = (((1,), (1,)), ((), ()))
TN = (((0,), (0,)), ((), ()))


def swiglu_back(gate, up, grad_hidden):
    sig = jax.nn.sigmoid(gate)
    hidden = (gate * sig * up).astype(BF16)
    grad_g = (grad_hidden * up * sig * (1.0 + gate * (1.0 - sig))).astype(BF16)
    grad_u = (grad_hidden * gate * sig).astype(BF16)
    return (hidden, grad_g, grad_u)


def exchange(
    n_row, n_col, nc, wire,
    tok_in, go_in, wg_in, wu_in, wd_in,
    gt_out, tok_out, go_out, h_out, g_out, u_out,
    x_v, wg_v, wu_v, wd_v, send_v, acc_v, mid_v, sum_v, res_v, gt_v, sib_v, peer_src, peer_v,
    w_sem, own_sem, out_sem,
    k_send, k_recv, s_send, s_recv,
    p_send, p_recv, m_recv, r_send, r_recv,
    t_send, t_recv, q_send, q_recv,
):
    row, col, dp = lax.axis_index("row"), lax.axis_index("col"), lax.axis_index("dp")
    rows, feats = tok_in.shape
    chunk = wg_v.shape[2]
    hid = nc * chunk
    half = n_row // 2
    left = row < half
    inner = jnp.where(left, row + 1, row - 1)
    outer = jnp.where(left, row - 1, row + 1)
    edge = jnp.logical_or(row == 0, row == n_row - 1)
    middle = jnp.logical_or(row == half - 1, row == half)
    off = dp * hid

    def block(j, core):
        return pl.ds(pl.multiple_of((j * 2 + core) * rows, 16), rows)

    def columns(c, base=0):
        return pl.ds(pl.multiple_of(base + c * chunk, 128), chunk)

    def weight_copies(c):
        return (
            pltpu.make_async_copy(wg_in.at[:, columns(c, off)], wg_v.at[c], w_sem.at[c, 0]),
            pltpu.make_async_copy(wu_in.at[:, columns(c, off)], wu_v.at[c], w_sem.at[c, 1]),
            pltpu.make_async_copy(wd_in.at[columns(c, off)], wd_v.at[c], w_sem.at[c, 2]),
        )

    own = [
        pltpu.make_async_copy(src, x_v.at[a, block(col, dp)], own_sem.at[a])
        for a, src in enumerate((tok_in, go_in))
    ]
    for copy in own:
        copy.start()

    def load(c, carry):
        for copy in weight_copies(c):
            copy.start()
        return carry

    lax.fori_loop(0, nc, load, 0)

    def col_at(k):
        return lax.rem(col + k, n_col)

    barrier = pltpu.get_barrier_semaphore()
    for k in range(1, n_col):
        pl.semaphore_signal(barrier, inc=1, device_id=(row, col_at(k), dp), device_id_type=MESH)
    pl.semaphore_signal(barrier, inc=1, device_id=(row, col, 1 - dp), device_id_type=MESH)
    pl.semaphore_signal(barrier, inc=1, device_id=(inner, col, dp), device_id_type=MESH)

    @pl.when(jnp.logical_not(edge))
    def _():
        pl.semaphore_signal(barrier, inc=1, device_id=(outer, col, dp), device_id_type=MESH)
        pl.semaphore_wait(barrier, n_col + 2)

    @pl.when(edge)
    def _():
        pl.semaphore_wait(barrier, n_col + 1)

    def to_peer(k, a):
        return pltpu.make_async_remote_copy(
            src_ref=(tok_in, go_in)[a],
            dst_ref=x_v.at[a, block(col, dp)],
            send_sem=k_send.at[k, a],
            recv_sem=k_recv.at[k, a],
            device_id=(row, col_at(k), dp),
            device_id_type=MESH,
        )

    def to_sibling(k, a):
        rows_of = block(col_at(n_col - k), dp)
        return pltpu.make_async_remote_copy(
            src_ref=(tok_in, go_in)[a] if k == 0 else x_v.at[a, rows_of],
            dst_ref=x_v.at[a, rows_of],
            send_sem=s_send.at[k, a],
            recv_sem=s_recv.at[k, a],
            device_id=(row, col, 1 - dp),
            device_id_type=MESH,
        )

    for a in range(2):
        for k in range(1, n_col):
            to_peer(k, a).start()
        to_sibling(0, a).start()
    for a in range(2):
        for k in range(1, n_col):
            to_peer(k, a).wait_recv()
            to_sibling(k, a).start()
    for copy in own:
        copy.wait()
    for a in range(2):
        for k in range(n_col):
            to_sibling(k, a).wait_recv()
    x_out = [
        pltpu.make_async_copy(x_v.at[a], dst, own_sem.at[a])
        for a, dst in enumerate((tok_out, go_out))
    ]
    for copy in x_out:
        copy.start()

    def sum_inwards(c, into_middle):
        return pltpu.make_async_remote_copy(
            src_ref=send_v.at[c],
            dst_ref=mid_v.at[c] if into_middle else acc_v.at[c],
            send_sem=p_send.at[c],
            recv_sem=m_recv.at[c] if into_middle else p_recv.at[c],
            device_id=(inner, col, dp),
            device_id_type=MESH,
        )

    def result_outwards(c):
        return pltpu.make_async_remote_copy(
            src_ref=res_v.at[c],
            dst_ref=res_v.at[c],
            send_sem=r_send.at[c],
            recv_sem=r_recv.at[c],
            device_id=(outer, col, dp),
            device_id_type=MESH,
        )

    def result_copies(c):
        return [
            pltpu.make_async_copy(res_v.at[c, i], dst.at[:, columns(c)], out_sem.at[c, i])
            for i, dst in enumerate((h_out, g_out, u_out))
        ]

    gt_v[...] = jnp.zeros_like(gt_v)

    def backward(c):
        for copy in result_copies(c):
            copy.start()
        gt_v[...] += lax.dot_general(
            res_v[c, 1], wg_v[c], NT, preferred_element_type=F32
        ) + lax.dot_general(res_v[c, 2], wu_v[c], NT, preferred_element_type=F32)

    def finish(c):
        sum_inwards(c, True).wait_recv()
        h, g, u = swiglu_back(*(sum_v[c, i] + mid_v[c, i].astype(F32) for i in range(3)))
        res_v[c, 0] = h
        res_v[c, 1] = g
        res_v[c, 2] = u
        if half > 1:
            result_outwards(c).start()
        backward(c)

    def forward(c, carry):
        for copy in weight_copies(c):
            copy.wait()
        sum_v[c, 0] = jnp.dot(x_v[0], wg_v[c], preferred_element_type=F32)
        sum_v[c, 1] = jnp.dot(x_v[0], wu_v[c], preferred_element_type=F32)
        sum_v[c, 2] = lax.dot_general(x_v[1], wd_v[c], NT, preferred_element_type=F32)

        if half > 1:

            @pl.when(jnp.logical_not(edge))
            def _():
                sum_inwards(c, False).wait_recv()
                sum_v[c] += acc_v[c].astype(F32)

        send_v[c] = sum_v[c].astype(wire)

        @pl.when(middle)
        def _():
            sum_inwards(c, True).start()

            @pl.when(c > 0)
            def _():
                finish(c - 1)

        @pl.when(jnp.logical_not(middle))
        def _():
            sum_inwards(c, False).start()

        return carry

    lax.fori_loop(0, nc, forward, 0)

    @pl.when(middle)
    def _():
        finish(nc - 1)

    if half > 1:

        @pl.when(jnp.logical_not(middle))
        def _():
            def take(c, carry):
                result_outwards(c).wait_recv()

                @pl.when(jnp.logical_not(edge))
                def _():
                    result_outwards(c).start()

                backward(c)
                return carry

            lax.fori_loop(0, nc, take, 0)

    def half_to_sibling(k):
        return pltpu.make_async_remote_copy(
            src_ref=gt_v.at[block(col_at(k), 1 - dp)],
            dst_ref=sib_v.at[k],
            send_sem=t_send.at[k],
            recv_sem=t_recv.at[k],
            device_id=(row, col, 1 - dp),
            device_id_type=MESH,
        )

    def block_to_owner(k):
        return pltpu.make_async_remote_copy(
            src_ref=peer_src.at[k],
            dst_ref=peer_v.at[k],
            send_sem=q_send.at[k],
            recv_sem=q_recv.at[k],
            device_id=(row, col_at(k), dp),
            device_id_type=MESH,
        )

    order = list(range(1, n_col)) + [0]
    for k in order:
        half_to_sibling(k).start()
    for k in order[:-1]:
        half_to_sibling(k).wait_recv()
        peer_src[k] = (gt_v[block(col_at(k), dp), :] + sib_v[k]).astype(wire)
        block_to_owner(k).start()
    half_to_sibling(0).wait_recv()
    total = gt_v[block(col, dp), :] + sib_v[0]
    for k in order[:-1]:
        block_to_owner(k).wait_recv()
        total = total + peer_v[k].astype(F32)
    gt_out[...] = total.astype(BF16)

    for k in order:
        half_to_sibling(k).wait_send()
    for k in order[:-1]:
        block_to_owner(k).wait_send()
    for a in range(2):
        x_out[a].wait()
        for k in range(n_col):
            to_sibling(k, a).wait_send()
            if k > 0:
                to_peer(k, a).wait_send()

    def drain(c, carry):
        for copy in result_copies(c):
            copy.wait()
        sum_inwards(c, False).wait_send()
        if half > 1:

            @pl.when(jnp.logical_not(edge))
            def _():
                result_outwards(c).wait_send()

        return carry

    lax.fori_loop(0, nc, drain, 0)


def outer_products(tok, go, h, g, u, gate_out, up_out, down_out):
    gate_out[...] = lax.dot_general(
        tok[...], g[...], TN, preferred_element_type=F32
    ).astype(BF16)
    up_out[...] = lax.dot_general(tok[...], u[...], TN, preferred_element_type=F32).astype(BF16)
    down_out[...] = lax.dot_general(h[...], go[...], TN, preferred_element_type=F32).astype(BF16)


def body(n_row, n_col, tokens, grad_out, gate_weight, up_weight, down_weight):
    rows, feats = tokens.shape
    panel = rows * n_col * 2
    hid = gate_weight.shape[1] // 2
    chunk = min(256, hid)
    nc = hid // chunk
    wire = BF16 if n_row <= 4 else F32
    anywhere = pl.BlockSpec(memory_space=pl.ANY)
    dma = pltpu.SemaphoreType.DMA
    grad_tokens, tok, go, h, g, u = pl.pallas_call(
        functools.partial(exchange, n_row, n_col, nc, wire),
        out_shape=[
            jax.ShapeDtypeStruct((rows, feats), BF16),
            jax.ShapeDtypeStruct((panel, feats), BF16),
            jax.ShapeDtypeStruct((panel, feats), BF16),
            jax.ShapeDtypeStruct((panel, hid), BF16),
            jax.ShapeDtypeStruct((panel, hid), BF16),
            jax.ShapeDtypeStruct((panel, hid), BF16),
        ],
        in_specs=[anywhere] * 5,
        out_specs=[pl.BlockSpec(memory_space=pltpu.VMEM)] + [anywhere] * 5,
        scratch_shapes=[
            pltpu.VMEM((2, panel, feats), BF16),
            pltpu.VMEM((nc, feats, chunk), BF16),
            pltpu.VMEM((nc, feats, chunk), BF16),
            pltpu.VMEM((nc, chunk, feats), BF16),
            pltpu.VMEM((nc, 3, panel, chunk), wire),
            pltpu.VMEM((nc, 3, panel, chunk), wire),
            pltpu.VMEM((nc, 3, panel, chunk), wire),
            pltpu.VMEM((nc, 3, panel, chunk), F32),
            pltpu.VMEM((nc, 3, panel, chunk), BF16),
            pltpu.VMEM((panel, feats), F32),
            pltpu.VMEM((n_col, rows, feats), F32),
            pltpu.VMEM((n_col, rows, feats), wire),
            pltpu.VMEM((n_col, rows, feats), wire),
            dma((nc, 3)), dma((2,)), dma((nc, 3)),
            dma((n_col, 2)), dma((n_col, 2)), dma((n_col, 2)), dma((n_col, 2)),
            dma((nc,)), dma((nc,)), dma((nc,)), dma((nc,)), dma((nc,)),
            dma((n_col,)), dma((n_col,)), dma((n_col,)), dma((n_col,)),
        ],
        compiler_params=pltpu.CompilerParams(
            collective_id=0, has_side_effects=True, vmem_limit_bytes=56 * 2**20
        ),
        name="exchange",
    )(tokens, grad_out, gate_weight, up_weight, down_weight)

    nb = max(1, feats // 256)
    whole = lambda i: (0, 0)
    cut = lambda i: (0, i)
    stack = lambda i: (i, 0)
    grad_gate, grad_up, grad_down = pl.pallas_call(
        outer_products,
        grid=(nb,),
        in_specs=[
            pl.BlockSpec((panel, feats // nb), cut),
            pl.BlockSpec((panel, feats), whole),
            pl.BlockSpec((panel, hid // nb), cut),
            pl.BlockSpec((panel, hid), whole),
            pl.BlockSpec((panel, hid), whole),
        ],
        out_specs=[
            pl.BlockSpec((feats // nb, hid), stack),
            pl.BlockSpec((feats // nb, hid), stack),
            pl.BlockSpec((hid // nb, feats), stack),
        ],
        out_shape=[
            jax.ShapeDtypeStruct((feats, hid), BF16),
            jax.ShapeDtypeStruct((feats, hid), BF16),
            jax.ShapeDtypeStruct((hid, feats), BF16),
        ],
        compiler_params=pltpu.CompilerParams(vmem_limit_bytes=40 * 2**20),
        name="outer_products",
    )(tok, go, h, g, u)
    return (grad_tokens, grad_gate, grad_up, grad_down)


def solution(mesh):
    in_specs = (
        P(("col", "dp"), "row"),
        P(("col", "dp"), "row"),
        P("row", "col"),
        P("row", "col"),
        P("col", "row"),
    )
    out_specs = (
        P(("col", "dp"), "row"),
        P("row", ("col", "dp")),
        P("row", ("col", "dp")),
        P(("col", "dp"), "row"),
    )
    run = functools.partial(body, mesh.shape["row"], mesh.shape["col"])
    return jax.shard_map(run, mesh=mesh, in_specs=in_specs, out_specs=out_specs, check_vma=False)
```

time: 264 us -> 89.5 us (0.34)
  waiting for transfers between devices: 117 us -> 0 us
  Pallas kernels: 0 us -> 81.5 us
  matrix products: 65.8 us -> 0 us
  blocking collectives: 37 us -> 0 us
  local copies, waits for them, and re-layouts: 24.6 us -> 6.67 us
  between operations: 14.1 us -> 0.65 us
  other arithmetic: 3.96 us -> 0 us
    psum x1 -> x0, waiting for transfers between devices: 117 us -> none  [body(): gate, up, grad_hidden = lax.psum((gate_part, up_part, hidden_part), 'row')]
    pallas_call x0 -> x2, Pallas kernels: none -> 81.5 us  [the longest x1 71 us: body(): pl.pallas_call(functools.partial(exchange, n_row, n_col, nc, wire), out_s...]
    dot_general x8 -> x0, matrix products: 65.8 us -> none  [the longest x1 11.9 us: body(): lax.dot_general(panel_grad, down_weight, contract_last, preferred_element...]
    all_gather x4 -> x0, blocking collectives: 24.2 us -> none  [the longest x1 9.5 us: body(): lax.all_gather(tokens, 'col', axis=0, tiled=True)]
    unnamed x6 -> x11, local copies, waits for them, and re-layouts: 24.5 us -> 6.67 us
    all_to_all x3 -> x0, blocking collectives: 12.8 us -> none  [the longest x1 4.49 us: body(): lax.all_to_all(grad_g, 'dp', split_axis=1, concat_axis=0, tiled=True)]
    convert_element_type x2 -> x0, other arithmetic: 3.96 us -> none  [the longest x1 2.42 us: swiglu_back(): hidden = (gate * sig * up).astype(jnp.bfloat16)]
  transfers between devices with their start and end apart: 2 -> 0, of which waited for: 1 -> 0; matrix products, arithmetic and copies ran while one was open for 16% -> 0% of each run, Pallas kernels for 0% -> 0%
where the time goes in v1:
time: 89.5 us; the launch traced here: 88.8 us
  Pallas kernels  81.5 us (91%)
  local copies, waits for them, and re-layouts  6.67 us (7%)
    pallas_call x1, Pallas kernels, body(): pl.pallas_call(functools.partial(exchange, n_row, n_col, nc, wire), out_s...  71 us
    pallas_call x1, Pallas kernels, body(): pl.pallas_call(outer_products, grid=(nb,), in_specs=[pl.BlockSpec((panel,...  10.5 us
    unnamed x11, local copies, waits for them, and re-layouts  6.67 us

profile of v1, /device:TPU:1, one launch (start us, length us, event | category | flops | bytes accessed | tf_op | source)
XLA Modules:
  0.0 88.8 jit_solution(11564626356602330551)
XLA Ops:
  0.6 71.0 %exchange.1 = (bf16[16,2048]{1,0:T(8,128)(2,1)}, bf16[128,2048]{1,0:T(8,128)(2,1)}, bf16[128,2048]{1,0:T(8,128)(2,1)}, bf16[128,2048]{1,0:T(8,128)(2,1)}, bf16[1...) custom-call(bf16[16,2048]{1,0:T(8,128)(2,1)} %tok_in.1, bf16[16,2048]{1,0:T(8,128)(2,1)} %go_in.1, ...), custom_call_target="tpu_custom_call" | custom-call | tf_op jit(solution)/shard_map/exchange/pallas_call | solution.py:307
  71.6 0.0 copy-start
  71.6 1.0 %copy-done = bf16[128,2048]{1,0:T(8,128)(2,1)S(1)} copy-done((bf16[128,2048]{1,0:T(8,128)(2,1)S(1)}, bf16[128,2048]{1,0:T(8,128)(2,1)}, u32[]{:S(2)}) %copy-start) | copy-done | bytes 524312
  72.7 0.0 copy-start.1
  72.7 1.0 %copy-done.1 = bf16[128,2048]{1,0:T(8,128)(2,1)S(1)} copy-done((bf16[128,2048]{1,0:T(8,128)(2,1)S(1)}, bf16[128,2048]{1,0:T(8,128)(2,1)}, u32[]{:S(2)}) %copy-start.1) | copy-done | bytes 524312
  73.7 0.0 copy-start.2
  73.7 1.0 %copy-done.2 = bf16[128,2048]{1,0:T(8,128)(2,1)S(1)} copy-done((bf16[128,2048]{1,0:T(8,128)(2,1)S(1)}, bf16[128,2048]{1,0:T(8,128)(2,1)}, u32[]{:S(2)}) %copy-start.2) | copy-done | bytes 524312
  74.8 0.0 copy-start.3
  74.8 1.0 %copy-done.3 = bf16[128,2048]{1,0:T(8,128)(2,1)S(1)} copy-done((bf16[128,2048]{1,0:T(8,128)(2,1)S(1)}, bf16[128,2048]{1,0:T(8,128)(2,1)}, u32[]{:S(2)}) %copy-start.3) | copy-done | bytes 524312
  75.8 0.0 copy-start.4
  75.8 1.0 %copy-done.4 = bf16[128,2048]{1,0:T(8,128)(2,1)S(1)} copy-done((bf16[128,2048]{1,0:T(8,128)(2,1)S(1)}, bf16[128,2048]{1,0:T(8,128)(2,1)}, u32[]{:S(2)}) %copy-start.4) | copy-done | bytes 524312
  76.8 10.5 %outer_products.1 = (bf16[2048,2048]{1,0:T(8,128)(2,1)}, bf16[2048,2048]{1,0:T(8,128)(2,1)}, bf16[2048,2048]{1,0:T(8,128)(2,1)}) custom-call(bf16[128,2048]{1,0:T(8,128)(2,1)S(1)} %copy-done, bf16[128,2048]{1,0:T(8,128)(2,1)S(1)} %copy-done.1, bf16[128,2048]{1,0:T(8,128)(2,1)S(1)} %copy-done.2, bf16[128,2048]{1,0:T(8,128)(2,1)S(1)} %copy-done.3, ...), custom_call_target="tpu_custom_call" | custom-call | tf_op jit(solution)/shard_map/outer_products/pallas_call | solution.py:348
  87.4 1.5 %copy.10 = bf16[16,2048]{1,0:T(8,128)(2,1)} copy(bf16[16,2048]{1,0:T(8,128)(2,1)} %get-tuple-element.26) | data formatting | bytes 131072
Async XLA Ops:
  71.6 1.0 %copy-start = (bf16[128,2048]{1,0:T(8,128)(2,1)S(1)}, bf16[128,2048]{1,0:T(8,128)(2,1)}, u32[]{:S(2)}) copy-start(bf16[128,2048]{1,0:T(8,128)(2,1)} %get-tuple-element.14.tok) | copy-start | bytes 1572868
  72.7 1.0 %copy-start.1 = (bf16[128,2048]{1,0:T(8,128)(2,1)S(1)}, bf16[128,2048]{1,0:T(8,128)(2,1)}, u32[]{:S(2)}) copy-start(bf16[128,2048]{1,0:T(8,128)(2,1)} %get-tuple-element.15.go) | copy-start | bytes 1572868
  73.7 1.0 %copy-start.2 = (bf16[128,2048]{1,0:T(8,128)(2,1)S(1)}, bf16[128,2048]{1,0:T(8,128)(2,1)}, u32[]{:S(2)}) copy-start(bf16[128,2048]{1,0:T(8,128)(2,1)} %get-tuple-element.16.h) | copy-start | bytes 1572868
  74.8 1.0 %copy-start.3 = (bf16[128,2048]{1,0:T(8,128)(2,1)S(1)}, bf16[128,2048]{1,0:T(8,128)(2,1)}, u32[]{:S(2)}) copy-start(bf16[128,2048]{1,0:T(8,128)(2,1)} %get-tuple-element.17.g) | copy-start | bytes 1572868
  75.8 1.0 %copy-start.4 = (bf16[128,2048]{1,0:T(8,128)(2,1)S(1)}, bf16[128,2048]{1,0:T(8,128)(2,1)}, u32[]{:S(2)}) copy-start(bf16[128,2048]{1,0:T(8,128)(2,1)} %get-tuple-element.18.u) | copy-start | bytes 1572868

commit v2 on v1

v2 whole, which is shorter than its diff:
```python
import functools

import jax
import jax.numpy as jnp
from jax import lax
from jax.experimental import pallas as pl
from jax.experimental.pallas import tpu as pltpu
from jax.sharding import PartitionSpec as P

MESH = pl.DeviceIdType.MESH
BF16 = jnp.bfloat16
F32 = jnp.float32
NT = (((1,), (1,)), ((), ()))


def swiglu_back(gate, up, grad_hidden):
    sig = jax.nn.sigmoid(gate)
    hidden = (gate * sig * up).astype(BF16)
    grad_g = (grad_hidden * up * sig * (1.0 + gate * (1.0 - sig))).astype(BF16)
    grad_u = (grad_hidden * gate * sig).astype(BF16)
    return (hidden, grad_g, grad_u)


def exchange(
    n_row, n_col, nc, ns, wire,
    tok_in, go_in, wg_in, wu_in, wd_in,
    gt_out, tok_out, go_out, h_out, g_out, u_out,
    x_v, wg_v, wu_v, wd_v, send_v, acc_v, mid_v, sum_v, res_v, gt_v, sib_v, peer_src, peer_v,
    turn_v, hid_v,
    w_sem, own_sem, out_sem,
    k_send, k_recv, s_send, s_recv,
    p_send, p_recv, m_recv, r_send, r_recv,
    t_send, t_recv, q_send, q_recv,
):
    row, col, dp = lax.axis_index("row"), lax.axis_index("col"), lax.axis_index("dp")
    rows, feats = tok_in.shape
    panel = x_v.shape[1]
    chunk = wg_v.shape[2]
    hid = nc * chunk
    half = n_row // 2
    left = row < half
    inner = jnp.where(left, row + 1, row - 1)
    outer = jnp.where(left, row - 1, row + 1)
    edge = jnp.logical_or(row == 0, row == n_row - 1)
    middle = jnp.logical_or(row == half - 1, row == half)
    off = dp * hid

    first = 2 * rows
    step = (panel - first) // ns
    units = [(0, first)] + [(first + i * step, step) for i in range(ns)]

    def block(k, core):
        return pl.ds(pl.multiple_of((k * 2 + core) * rows, 16), rows)

    def columns(c, base=0):
        return pl.ds(pl.multiple_of(base + c * chunk, 128), chunk)

    def weight_copies(c):
        return (
            pltpu.make_async_copy(wg_in.at[:, columns(c, off)], wg_v.at[c], w_sem.at[c, 0]),
            pltpu.make_async_copy(wu_in.at[:, columns(c, off)], wu_v.at[c], w_sem.at[c, 1]),
            pltpu.make_async_copy(wd_in.at[columns(c, off)], wd_v.at[c], w_sem.at[c, 2]),
        )

    own = [
        pltpu.make_async_copy(src, x_v.at[a, block(0, dp)], own_sem.at[a])
        for a, src in enumerate((tok_in, go_in))
    ]
    for copy in own:
        copy.start()

    def load(c, carry):
        for copy in weight_copies(c):
            copy.start()
        return carry

    lax.fori_loop(0, nc, load, 0)

    def col_at(k):
        return lax.rem(col + k, n_col)

    barrier = pltpu.get_barrier_semaphore()
    for k in range(1, n_col):
        pl.semaphore_signal(barrier, inc=1, device_id=(row, col_at(k), dp), device_id_type=MESH)
    pl.semaphore_signal(barrier, inc=1, device_id=(row, col, 1 - dp), device_id_type=MESH)
    pl.semaphore_signal(barrier, inc=1, device_id=(inner, col, dp), device_id_type=MESH)

    @pl.when(jnp.logical_not(edge))
    def _():
        pl.semaphore_signal(barrier, inc=1, device_id=(outer, col, dp), device_id_type=MESH)
        pl.semaphore_wait(barrier, n_col + 2)

    @pl.when(edge)
    def _():
        pl.semaphore_wait(barrier, n_col + 1)

    def to_peer(k, a):
        return pltpu.make_async_remote_copy(
            src_ref=(tok_in, go_in)[a],
            dst_ref=x_v.at[a, block(n_col - k, dp)],
            send_sem=k_send.at[k, a],
            recv_sem=k_recv.at[k, a],
            device_id=(row, col_at(k), dp),
            device_id_type=MESH,
        )

    def to_sibling(k, a):
        return pltpu.make_async_remote_copy(
            src_ref=(tok_in, go_in)[a] if k == 0 else x_v.at[a, block(k, dp)],
            dst_ref=x_v.at[a, block(k, dp)],
            send_sem=s_send.at[k, a],
            recv_sem=s_recv.at[k, a],
            device_id=(row, col, 1 - dp),
            device_id_type=MESH,
        )

    for a in range(2):
        to_sibling(0, a).start()
    for a in range(2):
        for k in range(1, n_col):
            to_peer(k, a).start()

    def part(ref, c, t):
        return ref.at[c, :, pl.ds(*units[t])]

    def sum_inwards(c, t, into_middle):
        return pltpu.make_async_remote_copy(
            src_ref=part(send_v, c, t),
            dst_ref=part(mid_v if into_middle else acc_v, c, t),
            send_sem=p_send.at[c, t],
            recv_sem=(m_recv if into_middle else p_recv).at[c, t],
            device_id=(inner, col, dp),
            device_id_type=MESH,
        )

    def result_outwards(c, t):
        return pltpu.make_async_remote_copy(
            src_ref=part(res_v, c, t),
            dst_ref=part(res_v, c, t),
            send_sem=r_send.at[c, t],
            recv_sem=r_recv.at[c, t],
            device_id=(outer, col, dp),
            device_id_type=MESH,
        )

    def result_copies(c):
        return [
            pltpu.make_async_copy(hid_v.at[c], h_out.at[columns(c)], out_sem.at[c, 0]),
            pltpu.make_async_copy(res_v.at[c, 1], g_out.at[:, columns(c)], out_sem.at[c, 1]),
            pltpu.make_async_copy(res_v.at[c, 2], u_out.at[:, columns(c)], out_sem.at[c, 2]),
        ]

    gt_v[...] = jnp.zeros_like(gt_v)

    def backward(c):
        hid_v[c] = res_v[c, 0].T
        for copy in result_copies(c):
            copy.start()
        gt_v[...] += lax.dot_general(
            res_v[c, 1], wg_v[c], NT, preferred_element_type=F32
        ) + lax.dot_general(res_v[c, 2], wu_v[c], NT, preferred_element_type=F32)

    def finish(c, t):
        sum_inwards(c, t, True).wait_recv()
        at = pl.ds(*units[t])
        h, g, u = swiglu_back(*(sum_v[c, i, at] + mid_v[c, i, at].astype(F32) for i in range(3)))
        res_v[c, 0, at] = h
        res_v[c, 1, at] = g
        res_v[c, 2, at] = u
        if half > 1:
            result_outwards(c, t).start()
        if t == ns:
            backward(c)

    def forward(c, start, count):
        at = pl.ds(start, count)
        sum_v[c, 0, at] = jnp.dot(x_v[0, at], wg_v[c], preferred_element_type=F32)
        sum_v[c, 1, at] = jnp.dot(x_v[0, at], wu_v[c], preferred_element_type=F32)
        sum_v[c, 2, at] = lax.dot_general(x_v[1, at], wd_v[c], NT, preferred_element_type=F32)

    def send_on(c, t, then):
        at = pl.ds(*units[t])
        if half > 1:

            @pl.when(jnp.logical_not(edge))
            def _():
                sum_inwards(c, t, False).wait_recv()
                sum_v[c, :, at] += acc_v[c, :, at].astype(F32)

        send_v[c, :, at] = sum_v[c, :, at].astype(wire)

        @pl.when(middle)
        def _():
            sum_inwards(c, t, True).start()
            then()

        @pl.when(jnp.logical_not(middle))
        def _():
            sum_inwards(c, t, False).start()

    for copy in own:
        copy.wait()
    for a in range(2):
        to_sibling(0, a).wait_recv()

    def near(c, carry):
        for copy in weight_copies(c):
            copy.wait()
        forward(c, 0, first)

        def then():
            @pl.when(c > 1)
            def _():
                finish(c - 2, 0)

        send_on(c, 0, then)

        @pl.when(c == nc - 2)
        def _():
            for a in range(2):
                for k in range(1, n_col):
                    to_peer(n_col - k, a).wait_recv()
                    to_sibling(k, a).start()

        return carry

    lax.fori_loop(0, nc, near, 0)

    for a in range(2):
        for k in range(1, n_col):
            to_sibling(k, a).wait_recv()

    def far(c, carry):
        forward(c, first, panel - first)
        for t in range(1, ns + 1):

            def then(t=t):
                if t > 2:
                    finish(c, t - 2)
                else:

                    @pl.when(c == 0)
                    def _():
                        finish(nc - 3 + t, 0)

                    @pl.when(c > 0)
                    def _():
                        finish(c - 1, ns - 2 + t)

            send_on(c, t, then)
        return carry

    lax.fori_loop(0, nc, far, 0)

    turn_v[...] = x_v[0].T
    x_out = [
        pltpu.make_async_copy(turn_v, tok_out, own_sem.at[0]),
        pltpu.make_async_copy(x_v.at[1], go_out, own_sem.at[1]),
    ]
    for copy in x_out:
        copy.start()

    @pl.when(middle)
    def _():
        finish(nc - 1, ns - 1)
        finish(nc - 1, ns)

    if half > 1:

        @pl.when(jnp.logical_not(middle))
        def _():
            def take(c, t):
                result_outwards(c, t).wait_recv()

                @pl.when(jnp.logical_not(edge))
                def _():
                    result_outwards(c, t).start()

            def take_near(c, carry):
                take(c, 0)
                return carry

            def take_far(c, carry):
                for t in range(1, ns + 1):
                    take(c, t)
                backward(c)
                return carry

            lax.fori_loop(0, nc, take_near, 0)
            lax.fori_loop(0, nc, take_far, 0)

    def half_to_sibling(k):
        return pltpu.make_async_remote_copy(
            src_ref=gt_v.at[block(k, 1 - dp)],
            dst_ref=sib_v.at[k],
            send_sem=t_send.at[k],
            recv_sem=t_recv.at[k],
            device_id=(row, col, 1 - dp),
            device_id_type=MESH,
        )

    def block_to_owner(k):
        return pltpu.make_async_remote_copy(
            src_ref=peer_src.at[k],
            dst_ref=peer_v.at[k],
            send_sem=q_send.at[k],
            recv_sem=q_recv.at[k],
            device_id=(row, col_at(k), dp),
            device_id_type=MESH,
        )

    order = list(range(1, n_col)) + [0]
    for k in order:
        half_to_sibling(k).start()
    for k in order[:-1]:
        half_to_sibling(k).wait_recv()
        peer_src[k] = (gt_v[block(k, dp), :] + sib_v[k]).astype(wire)
        block_to_owner(k).start()
    half_to_sibling(0).wait_recv()
    total = gt_v[block(0, dp), :] + sib_v[0]
    for k in order[:-1]:
        block_to_owner(k).wait_recv()
        total = total + peer_v[k].astype(F32)
    gt_out[...] = total.astype(BF16)

    for k in order:
        half_to_sibling(k).wait_send()
    for k in order[:-1]:
        block_to_owner(k).wait_send()
    for a in range(2):
        x_out[a].wait()
        for k in range(n_col):
            to_sibling(k, a).wait_send()
            if k > 0:
                to_peer(k, a).wait_send()

    def drain(c, carry):
        for copy in result_copies(c):
            copy.wait()
        for t in range(ns + 1):
            sum_inwards(c, t, False).wait_send()
            if half > 1:

                @pl.when(jnp.logical_not(edge))
                def _():
                    result_outwards(c, t).wait_send()

        return carry

    lax.fori_loop(0, nc, drain, 0)


def outer_products(grad_in, tok, go, h, g, u, grad_tokens, gate_out, up_out, down_out):
    @pl.when(pl.program_id(0) == 0)
    def _():
        grad_tokens[...] = grad_in[...]

    gate_out[...] = jnp.dot(tok[...], g[...], preferred_element_type=F32).astype(BF16)
    up_out[...] = jnp.dot(tok[...], u[...], preferred_element_type=F32).astype(BF16)
    down_out[...] = jnp.dot(h[...], go[...], preferred_element_type=F32).astype(BF16)


def body(n_row, n_col, tokens, grad_out, gate_weight, up_weight, down_weight):
    rows, feats = tokens.shape
    panel = rows * n_col * 2
    hid = gate_weight.shape[1] // 2
    chunk = min(256, hid // 2)
    nc = hid // chunk
    ns = 3 if (panel - 2 * rows) % 48 == 0 else 2
    wire = BF16 if n_row <= 4 else F32
    anywhere = pl.BlockSpec(memory_space=pl.ANY)
    dma = pltpu.SemaphoreType.DMA
    grad_in, tok, go, h, g, u = pl.pallas_call(
        functools.partial(exchange, n_row, n_col, nc, ns, wire),
        out_shape=[
            jax.ShapeDtypeStruct((rows, feats), BF16),
            jax.ShapeDtypeStruct((feats, panel), BF16),
            jax.ShapeDtypeStruct((panel, feats), BF16),
            jax.ShapeDtypeStruct((hid, panel), BF16),
            jax.ShapeDtypeStruct((panel, hid), BF16),
            jax.ShapeDtypeStruct((panel, hid), BF16),
        ],
        in_specs=[anywhere] * 5,
        out_specs=[pl.BlockSpec(memory_space=pltpu.VMEM)] + [anywhere] * 5,
        scratch_shapes=[
            pltpu.VMEM((2, panel, feats), BF16),
            pltpu.VMEM((nc, feats, chunk), BF16),
            pltpu.VMEM((nc, feats, chunk), BF16),
            pltpu.VMEM((nc, chunk, feats), BF16),
            pltpu.VMEM((nc, 3, panel, chunk), wire),
            pltpu.VMEM((nc, 3, panel, chunk), wire),
            pltpu.VMEM((nc, 3, panel, chunk), wire),
            pltpu.VMEM((nc, 3, panel, chunk), F32),
            pltpu.VMEM((nc, 3, panel, chunk), BF16),
            pltpu.VMEM((panel, feats), F32),
            pltpu.VMEM((n_col, rows, feats), F32),
            pltpu.VMEM((n_col, rows, feats), wire),
            pltpu.VMEM((n_col, rows, feats), wire),
            pltpu.VMEM((feats, panel), BF16),
            pltpu.VMEM((nc, chunk, panel), BF16),
            dma((nc, 3)), dma((2,)), dma((nc, 3)),
            dma((n_col, 2)), dma((n_col, 2)), dma((n_col, 2)), dma((n_col, 2)),
            dma((nc, ns + 1)), dma((nc, ns + 1)), dma((nc, ns + 1)),
            dma((nc, ns + 1)), dma((nc, ns + 1)),
            dma((n_col,)), dma((n_col,)), dma((n_col,)), dma((n_col,)),
        ],
        compiler_params=pltpu.CompilerParams(
            collective_id=0, has_side_effects=True, vmem_limit_bytes=60 * 2**20
        ),
        name="exchange",
    )(tokens, grad_out, gate_weight, up_weight, down_weight)

    nb = max(1, hid // 256)
    whole = lambda i: (0, 0)
    cut = lambda i: (0, i)
    grads = pl.pallas_call(
        outer_products,
        grid=(nb,),
        in_specs=[
            pl.BlockSpec((rows, feats), whole),
            pl.BlockSpec((feats, panel), whole),
            pl.BlockSpec((panel, feats // nb), cut),
            pl.BlockSpec((hid, panel), whole),
            pl.BlockSpec((panel, hid // nb), cut),
            pl.BlockSpec((panel, hid // nb), cut),
        ],
        out_specs=[
            pl.BlockSpec((rows, feats), whole),
            pl.BlockSpec((feats, hid // nb), cut),
            pl.BlockSpec((feats, hid // nb), cut),
            pl.BlockSpec((hid, feats // nb), cut),
        ],
        out_shape=[
            jax.ShapeDtypeStruct((rows, feats), BF16),
            jax.ShapeDtypeStruct((feats, hid), BF16),
            jax.ShapeDtypeStruct((feats, hid), BF16),
            jax.ShapeDtypeStruct((hid, feats), BF16),
        ],
        compiler_params=pltpu.CompilerParams(vmem_limit_bytes=63 * 2**20),
        name="outer_products",
    )(grad_in, tok, go, h, g, u)
    return tuple(grads)


def solution(mesh):
    in_specs = (
        P(("col", "dp"), "row"),
        P(("col", "dp"), "row"),
        P("row", "col"),
        P("row", "col"),
        P("col", "row"),
    )
    out_specs = (
        P(("col", "dp"), "row"),
        P("row", ("col", "dp")),
        P("row", ("col", "dp")),
        P(("col", "dp"), "row"),
    )
    run = functools.partial(body, mesh.shape["row"], mesh.shape["col"])
    return jax.shard_map(run, mesh=mesh, in_specs=in_specs, out_specs=out_specs, check_vma=False)
```

time: 89.5 us -> 79 us (0.88)
  local copies, waits for them, and re-layouts: 6.67 us -> 0 us
  Pallas kernels: 81.5 us -> 77.9 us
    unnamed x11 -> x0, local copies, waits for them, and re-layouts: 6.67 us -> none
    pallas_call x2, Pallas kernels: 81.5 us -> 77.9 us  [the longest x1 66.3 us: body(): pl.pallas_call(functools.partial(exchange, n_row, n_col, nc, ns, wire), o...]
where the time goes in v2:
time: 79 us; the launch traced here: 78.5 us
  Pallas kernels  77.9 us (99%)
    pallas_call x1, Pallas kernels, body(): pl.pallas_call(functools.partial(exchange, n_row, n_col, nc, ns, wire), o...  66.3 us
    pallas_call x1, Pallas kernels, body(): pl.pallas_call(outer_products, grid=(nb,), in_specs=[pl.BlockSpec((rows,...  11.6 us

profile of v2, /device:TPU:1, one launch (start us, length us, event | category | flops | bytes accessed | tf_op | source)
XLA Modules:
  0.0 78.5 jit_solution(17561439023631765567)
XLA Ops:
  0.6 66.3 %exchange.1 = (bf16[16,2048]{1,0:T(8,128)(2,1)}, bf16[2048,128]{1,0:T(8,128)(2,1)}, bf16[128,2048]{1,0:T(8,128)(2,1)}, bf16[2048,128]{1,0:T(8,128)(2,1)}, bf16[1...) custom-call(bf16[16,2048]{1,0:T(8,128)(2,1)} %tok_in.1, bf16[16,2048]{1,0:T(8,128)(2,1)} %go_in.1, ...), custom_call_target="tpu_custom_call" | custom-call | tf_op jit(solution)/shard_map/exchange/pallas_call | solution.py:373
  67.0 11.6 %outer_products.1 = (bf16[16,2048]{1,0:T(8,128)(2,1)}, bf16[2048,2048]{1,0:T(8,128)(2,1)}, bf16[2048,2048]{1,0:T(8,128)(2,1)}, bf16[2048,2048]{1,0:T(8,128)(2,1)}) custom-call(bf16[16,2048]{1,0:T(8,128)(2,1)} %get-tuple-element.10.grad_in, bf16[2048,128]{1,0:T(8,128)(2,1)} %get-tuple-element.11.tok, bf16[128,2048]{1,0:T(8,128)(2,1)} %get-tuple-element.12.go, ...), custom_call_target="tpu_custom_call" | custom-call | tf_op jit(solution)/shard_map/outer_products/pallas_call | solution.py:416

commit v3 on v2

--- a/solution.py
+++ b/solution.py
@@ -10,7 +10,6 @@
 MESH = pl.DeviceIdType.MESH
 BF16 = jnp.bfloat16
 F32 = jnp.float32
-NT = (((1,), (1,)), ((), ()))
 
 
 def swiglu_back(gate, up, grad_hidden):
@@ -26,7 +25,7 @@
     tok_in, go_in, wg_in, wu_in, wd_in,
     gt_out, tok_out, go_out, h_out, g_out, u_out,
     x_v, wg_v, wu_v, wd_v, send_v, acc_v, mid_v, sum_v, res_v, gt_v, sib_v, peer_src, peer_v,
-    turn_v, hid_v,
+    turn_v, hid_v, near_v, far_v, gtt_v,
     w_sem, own_sem, out_sem,
     k_send, k_recv, s_send, s_recv,
     p_send, p_recv, m_recv, r_send, r_recv,
@@ -150,15 +149,15 @@
             pltpu.make_async_copy(res_v.at[c, 2], u_out.at[:, columns(c)], out_sem.at[c, 2]),
         ]
 
-    gt_v[...] = jnp.zeros_like(gt_v)
+    gtt_v[...] = jnp.zeros_like(gtt_v)
 
     def backward(c):
         hid_v[c] = res_v[c, 0].T
         for copy in result_copies(c):
             copy.start()
-        gt_v[...] += lax.dot_general(
-            res_v[c, 1], wg_v[c], NT, preferred_element_type=F32
-        ) + lax.dot_general(res_v[c, 2], wu_v[c], NT, preferred_element_type=F32)
+        gtt_v[...] += jnp.dot(
+            wg_v[c], res_v[c, 1].T, preferred_element_type=F32
+        ) + jnp.dot(wu_v[c], res_v[c, 2].T, preferred_element_type=F32)
 
     def finish(c, t):
         sum_inwards(c, t, True).wait_recv()
@@ -172,11 +171,19 @@
         if t == ns:
             backward(c)
 
-    def forward(c, start, count):
+    def turned(start, count):
+        x = x_v[1, pl.ds(start, count)]
+        fill = -count % 128
+        if fill:
+            x = jnp.concatenate([x, jnp.zeros((fill, feats), BF16)], axis=0)
+        return x.T
+
+    def forward(c, start, count, cotangents):
         at = pl.ds(start, count)
         sum_v[c, 0, at] = jnp.dot(x_v[0, at], wg_v[c], preferred_element_type=F32)
         sum_v[c, 1, at] = jnp.dot(x_v[0, at], wu_v[c], preferred_element_type=F32)
-        sum_v[c, 2, at] = lax.dot_general(x_v[1, at], wd_v[c], NT, preferred_element_type=F32)
+        back = jnp.dot(wd_v[c], cotangents[...], preferred_element_type=F32)
+        sum_v[c, 2, at] = back.T[:count]
 
     def send_on(c, t, then):
         at = pl.ds(*units[t])
@@ -203,15 +210,17 @@
     for a in range(2):
         to_sibling(0, a).wait_recv()
 
+    near_v[...] = turned(0, first)
+
     def near(c, carry):
         for copy in weight_copies(c):
             copy.wait()
-        forward(c, 0, first)
+        forward(c, 0, first, near_v)
 
         def then():
-            @pl.when(c > 1)
+            @pl.when(c >= ns)
             def _():
-                finish(c - 2, 0)
+                finish(c - ns, 0)
 
         send_on(c, 0, then)
 
@@ -230,22 +239,20 @@
         for k in range(1, n_col):
             to_sibling(k, a).wait_recv()
 
+    far_v[...] = turned(first, panel - first)
+
     def far(c, carry):
-        forward(c, first, panel - first)
+        forward(c, first, panel - first, far_v)
         for t in range(1, ns + 1):
 
             def then(t=t):
-                if t > 2:
-                    finish(c, t - 2)
-                else:
-
-                    @pl.when(c == 0)
-                    def _():
-                        finish(nc - 3 + t, 0)
-
-                    @pl.when(c > 0)
-                    def _():
-                        finish(c - 1, ns - 2 + t)
+                @pl.when(c == 0)
+                def _():
+                    finish(nc - ns - 1 + t, 0)
+
+                @pl.when(c > 0)
+                def _():
+                    finish(c - 1, t)
 
             send_on(c, t, then)
         return carry
@@ -262,8 +269,8 @@
 
     @pl.when(middle)
     def _():
-        finish(nc - 1, ns - 1)
-        finish(nc - 1, ns)
+        for t in range(1, ns + 1):
+            finish(nc - 1, t)
 
     if half > 1:
 
@@ -288,6 +295,8 @@
 
             lax.fori_loop(0, nc, take_near, 0)
             lax.fori_loop(0, nc, take_far, 0)
+
+    gt_v[...] = gtt_v[...].T
 
     def half_to_sibling(k):
         return pltpu.make_async_remote_copy(
@@ -355,16 +364,18 @@
     def _():
         grad_tokens[...] = grad_in[...]
 
-    gate_out[...] = jnp.dot(tok[...], g[...], preferred_element_type=F32).astype(BF16)
-    up_out[...] = jnp.dot(tok[...], u[...], preferred_element_type=F32).astype(BF16)
-    down_out[...] = jnp.dot(h[...], go[...], preferred_element_type=F32).astype(BF16)
+    for left, right, out in ((tok, g, gate_out), (tok, u, up_out), (h, go, down_out)):
+        width = min(512, right.shape[1])
+        for start in range(0, right.shape[1], width):
+            at = pl.ds(start, width)
+            out[:, at] = jnp.dot(left[...], right[:, at], preferred_element_type=F32).astype(BF16)
 
 
 def body(n_row, n_col, tokens, grad_out, gate_weight, up_weight, down_weight):
     rows, feats = tokens.shape
     panel = rows * n_col * 2
     hid = gate_weight.shape[1] // 2
-    chunk = min(256, hid // 2)
+    chunk = min(256, hid // 4)
     nc = hid // chunk
     ns = 3 if (panel - 2 * rows) % 48 == 0 else 2
     wire = BF16 if n_row <= 4 else F32
@@ -398,6 +409,9 @@
             pltpu.VMEM((n_col, rows, feats), wire),
             pltpu.VMEM((feats, panel), BF16),
             pltpu.VMEM((nc, chunk, panel), BF16),
+            pltpu.VMEM((feats, -(-2 * rows // 128) * 128), BF16),
+            pltpu.VMEM((feats, -(-(panel - 2 * rows) // 128) * 128), BF16),
+            pltpu.VMEM((feats, panel), F32),
             dma((nc, 3)), dma((2,)), dma((nc, 3)),
             dma((n_col, 2)), dma((n_col, 2)), dma((n_col, 2)), dma((n_col, 2)),
             dma((nc, ns + 1)), dma((nc, ns + 1)), dma((nc, ns + 1)),
@@ -412,23 +426,23 @@
 
     nb = max(1, hid // 256)
     whole = lambda i: (0, 0)
-    cut = lambda i: (0, i)
+    stack = lambda i: (i, 0)
     grads = pl.pallas_call(
         outer_products,
         grid=(nb,),
         in_specs=[
             pl.BlockSpec((rows, feats), whole),
-            pl.BlockSpec((feats, panel), whole),
-            pl.BlockSpec((panel, feats // nb), cut),
-            pl.BlockSpec((hid, panel), whole),
-            pl.BlockSpec((panel, hid // nb), cut),
-            pl.BlockSpec((panel, hid // nb), cut),
+            pl.BlockSpec((feats // nb, panel), stack),
+            pl.BlockSpec((panel, feats), whole),
+            pl.BlockSpec((hid // nb, panel), stack),
+            pl.BlockSpec((panel, hid), whole),
+            pl.BlockSpec((panel, hid), whole),
         ],
         out_specs=[
             pl.BlockSpec((rows, feats), whole),
-            pl.BlockSpec((feats, hid // nb), cut),
-            pl.BlockSpec((feats, hid // nb), cut),
-            pl.BlockSpec((hid, feats // nb), cut),
+            pl.BlockSpec((feats // nb, hid), stack),
+            pl.BlockSpec((feats // nb, hid), stack),
+            pl.BlockSpec((hid // nb, feats), stack),
         ],
         out_shape=[
             jax.ShapeDtypeStruct((rows, feats), BF16),

time: 79 us -> 72.3 us (0.915)
  Pallas kernels: 77.9 us -> 71.3 us
    pallas_call x1, Pallas kernels: 66.3 us -> 59.5 us  [body(): pl.pallas_call(functools.partial(exchange, n_row, n_col, nc, ns, wire), o...]
where the time goes in v3:
time: 72.3 us; the launch traced here: 71.9 us
  Pallas kernels  71.3 us (99%)
    pallas_call x1, Pallas kernels, body(): pl.pallas_call(functools.partial(exchange, n_row, n_col, nc, ns, wire), o...  59.5 us
    pallas_call x1, Pallas kernels, body(): pl.pallas_call(outer_products, grid=(nb,), in_specs=[pl.BlockSpec((rows,...  11.8 us

profile of v3, /device:TPU:1, one launch (start us, length us, event | category | flops | bytes accessed | tf_op | source)
XLA Modules:
  0.0 71.9 jit_solution(6212822938534024772)
XLA Ops:
  0.6 59.5 %exchange.1 = (bf16[16,2048]{1,0:T(8,128)(2,1)}, bf16[2048,128]{1,0:T(8,128)(2,1)}, bf16[128,2048]{1,0:T(8,128)(2,1)}, bf16[2048,128]{1,0:T(8,128)(2,1)}, bf16[1...) custom-call(bf16[16,2048]{1,0:T(8,128)(2,1)} %tok_in.1, bf16[16,2048]{1,0:T(8,128)(2,1)} %go_in.1, ...), custom_call_target="tpu_custom_call" | custom-call | tf_op jit(solution)/shard_map/exchange/pallas_call | solution.py:384
  60.2 11.8 %outer_products.1 = (bf16[16,2048]{1,0:T(8,128)(2,1)}, bf16[2048,2048]{1,0:T(8,128)(2,1)}, bf16[2048,2048]{1,0:T(8,128)(2,1)}, bf16[2048,2048]{1,0:T(8,128)(2,1)}) custom-call(bf16[16,2048]{1,0:T(8,128)(2,1)} %get-tuple-element.10.grad_in, bf16[2048,128]{1,0:T(8,128)(2,1)} %get-tuple-element.11.tok, bf16[128,2048]{1,0:T(8,128)(2,1)} %get-tuple-element.12.go, ...), custom_call_target="tpu_custom_call" | custom-call | tf_op jit(solution)/shard_map/outer_products/pallas_call | solution.py:430

commit v4 on v3

--- a/solution.py
+++ b/solution.py
@@ -68,12 +68,9 @@
     for copy in own:
         copy.start()
 
-    def load(c, carry):
+    for c in range(2):
         for copy in weight_copies(c):
             copy.start()
-        return carry
-
-    lax.fori_loop(0, nc, load, 0)
 
     def col_at(k):
         return lax.rem(col + k, n_col)
@@ -213,6 +210,11 @@
     near_v[...] = turned(0, first)
 
     def near(c, carry):
+        @pl.when(c + 2 < nc)
+        def _():
+            for copy in weight_copies(c + 2):
+                copy.start()
+
         for copy in weight_copies(c):
             copy.wait()
         forward(c, 0, first, near_v)
@@ -359,16 +361,64 @@
     lax.fori_loop(0, nc, drain, 0)
 
 
-def outer_products(grad_in, tok, go, h, g, u, grad_tokens, gate_out, up_out, down_out):
-    @pl.when(pl.program_id(0) == 0)
-    def _():
-        grad_tokens[...] = grad_in[...]
-
-    for left, right, out in ((tok, g, gate_out), (tok, u, up_out), (h, go, down_out)):
+def outer_products(
+    nb,
+    grad_in, tok, go, h, g, u,
+    grad_tokens, gate_out, up_out, down_out,
+    tok_v, go_v, h_v, g_v, u_v, gate_v, up_v, down_v, in_sem, out_sem, pass_sem,
+):
+    through = pltpu.make_async_copy(grad_in, grad_tokens, pass_sem)
+    loads = [
+        pltpu.make_async_copy(src, dst, in_sem.at[i])
+        for i, (src, dst) in enumerate(
+            ((tok, tok_v), (g, g_v), (u, u_v), (h, h_v), (go, go_v))
+        )
+    ]
+    for copy in loads:
+        copy.start()
+    through.start()
+
+    def stores(k, i):
+        staged, out = ((gate_v, gate_out), (up_v, up_out), (down_v, down_out))[k]
+        count = out.shape[0] // (2 * nb)
+        for part in range(2):
+            at = pl.ds(pl.multiple_of((2 * i + part) * count, count), count)
+            yield pltpu.make_async_copy(staged.at[at], out.at[at], out_sem.at[k, i, part])
+
+    def product(k, left, right, staged):
+        count = left.shape[0] // nb
         width = min(512, right.shape[1])
-        for start in range(0, right.shape[1], width):
-            at = pl.ds(start, width)
-            out[:, at] = jnp.dot(left[...], right[:, at], preferred_element_type=F32).astype(BF16)
+
+        def step(i, carry):
+            at = pl.ds(pl.multiple_of(i * count, count), count)
+            for start in range(0, right.shape[1], width):
+                cols = pl.ds(start, width)
+                staged[at, cols] = jnp.dot(
+                    left[at, :], right[:, cols], preferred_element_type=F32
+                ).astype(BF16)
+            for copy in stores(k, i):
+                copy.start()
+            return carry
+
+        lax.fori_loop(0, nb, step, 0)
+
+    loads[0].wait()
+    loads[1].wait()
+    product(0, tok_v, g_v, gate_v)
+    loads[2].wait()
+    product(1, tok_v, u_v, up_v)
+    loads[3].wait()
+    loads[4].wait()
+    product(2, h_v, go_v, down_v)
+
+    def drain(i, carry):
+        for k in range(3):
+            for copy in stores(k, i):
+                copy.wait()
+        return carry
+
+    lax.fori_loop(0, nb, drain, 0)
+    through.wait()
 
 
 def body(n_row, n_col, tokens, grad_out, gate_weight, up_weight, down_weight):
@@ -425,24 +475,20 @@
     )(tokens, grad_out, gate_weight, up_weight, down_weight)
 
     nb = max(1, hid // 256)
-    whole = lambda i: (0, 0)
-    stack = lambda i: (i, 0)
     grads = pl.pallas_call(
-        outer_products,
-        grid=(nb,),
-        in_specs=[
-            pl.BlockSpec((rows, feats), whole),
-            pl.BlockSpec((feats // nb, panel), stack),
-            pl.BlockSpec((panel, feats), whole),
-            pl.BlockSpec((hid // nb, panel), stack),
-            pl.BlockSpec((panel, hid), whole),
-            pl.BlockSpec((panel, hid), whole),
-        ],
-        out_specs=[
-            pl.BlockSpec((rows, feats), whole),
-            pl.BlockSpec((feats // nb, hid), stack),
-            pl.BlockSpec((feats // nb, hid), stack),
-            pl.BlockSpec((hid // nb, feats), stack),
+        functools.partial(outer_products, nb),
+        in_specs=[anywhere] * 6,
+        out_specs=[anywhere] * 4,
+        scratch_shapes=[
+            pltpu.VMEM((feats, panel), BF16),
+            pltpu.VMEM((panel, feats), BF16),
+            pltpu.VMEM((hid, panel), BF16),
+            pltpu.VMEM((panel, hid), BF16),
+            pltpu.VMEM((panel, hid), BF16),
+            pltpu.VMEM((feats, hid), BF16),
+            pltpu.VMEM((feats, hid), BF16),
+            pltpu.VMEM((hid, feats), BF16),
+            dma((5,)), dma((3, nb, 2)), dma,
         ],
         out_shape=[
             jax.ShapeDtypeStruct((rows, feats), BF16),

time: 72.3 us -> 73.6 us (1.018)
  Pallas kernels: 71.3 us -> 72.8 us
    pallas_call x1, Pallas kernels: 11.8 us -> 12.7 us  [body(): pl.pallas_call(functools.partial(outer_products, nb), in_specs=[anywhere]...]
where the time goes in v4:
time: 73.6 us; the launch traced here: 73.4 us
  Pallas kernels  72.8 us (99%)
    pallas_call x1, Pallas kernels, body(): pl.pallas_call(functools.partial(exchange, n_row, n_col, nc, ns, wire), o...  60 us
    pallas_call x1, Pallas kernels, body(): pl.pallas_call(functools.partial(outer_products, nb), in_specs=[anywhere]...  12.7 us

profile of v4, /device:TPU:1, one launch (start us, length us, event | category | flops | bytes accessed | tf_op | source)
XLA Modules:
  0.0 73.4 jit_solution(11173210523664134072)
XLA Ops:
  0.6 60.0 %exchange.1 = (bf16[16,2048]{1,0:T(8,128)(2,1)}, bf16[2048,128]{1,0:T(8,128)(2,1)}, bf16[128,2048]{1,0:T(8,128)(2,1)}, bf16[2048,128]{1,0:T(8,128)(2,1)}, bf16[1...) custom-call(bf16[16,2048]{1,0:T(8,128)(2,1)} %tok_in.1, bf16[16,2048]{1,0:T(8,128)(2,1)} %go_in.1, ...), custom_call_target="tpu_custom_call" | custom-call | tf_op jit(solution)/shard_map/exchange/pallas_call | solution.py:434
  60.7 12.7 %outer_products.1 = (bf16[16,2048]{1,0:T(8,128)(2,1)}, bf16[2048,2048]{1,0:T(8,128)(2,1)}, bf16[2048,2048]{1,0:T(8,128)(2,1)}, bf16[2048,2048]{1,0:T(8,128)(2,1)}) custom-call(bf16[16,2048]{1,0:T(8,128)(2,1)} %get-tuple-element.10.grad_in, bf16[2048,128]{1,0:T(8,128)(2,1)} %get-tuple-element.11.tok, bf16[128,2048]{1,0:T(8,128)(2,1)} %get-tuple-element.12.go, ...), custom_call_target="tpu_custom_call" | custom-call | tf_op jit(solution)/shard_map/outer_products/pallas_call | solution.py:478
